TPU v7x, 128 devices: a whole 4x4x4 slice. The times are simulated.
128 devices in a mesh: gx: 8 (over x, core), gy: 16 (over z, y).
Axes of the slice: x: 4, y: 4, z: 4, core: 2. Of those that a mesh axis runs over, the one named last changes fastest.
Arguments:
- feats: bfloat16 [64, 524288], P(None, ('gx', 'gy')), may hold values from -6 to 6
- face_rows: int32 [128, 4, 128], P(('gx', 'gy')), may hold values from 0 to 4095
- neighbours: int32 [27, 524288], P(None, ('gx', 'gy')), may hold values from -1 to 4607, as said below
- z_dest: int32 [2, 524288], P(None, ('gx', 'gy')), may hold values from 0 to 4095, as said below
- h_dest: int32 [2, 524288], P(None, ('gx', 'gy')), may hold values from 0 to 4095, as said below
- conv_weight: bfloat16 [27, 64, 64], replicated, may hold values from -0.15625 to 0.15625
- qkv_weight: bfloat16 [2, 64, 192], replicated, may hold values from -4 to 4
- out_weight: bfloat16 [2, 64, 64], replicated, may hold values from -0.75 to 0.75
- up_weight: bfloat16 [2, 64, 256], replicated, may hold values from -0.75 to 0.75
- down_weight: bfloat16 [2, 256, 64], replicated, may hold values from -0.375 to 0.375
- norm_gains: float32 [5, 64], replicated, may hold values from 0.1 to 1.9
Outputs:
- result: bfloat16 [64, 524288], P(None, ('gx', 'gy'))
Inputs may be any that keep to these rules, and one draw needn't show every extreme that they name: `neighbours`: entry 13 of each point is the point itself; other entries are -1 (no neighbour), a local point 0 to 4095, or 4096 + f * 128 + r for row r of the f-th block of face points in extended. `z_dest`: row 0 is the owner device, row 1 the slot in the owner's patch buffer; all (owner, slot) pairs are distinct, so every device owns 4096 points. The points of one device go 48 to each of half of the devices and a third of 48 to each of the other half. `h_dest`: same form and counts as z_dest, for the Hilbert order. `face_rows`: rows 0 to 3 list points of the tile's lower x, upper x, lower y and upper y faces.
All inputs are finite; a program needn't handle non-finite values.
Results may differ from a plain program's by a relative error of at most 0.019.
The roundings to bfloat16 on the way count: a program that leaves them out, or rounds other values in their place, can miss the bound.
Values may be sent and summed in bfloat16 or wider, within the bound.
No kernel may reach another device: no remote copies, remote signals or barrier semaphores. Data moves between devices by JAX's collectives and lax.ppermute only.
A program may use at most 128 MiB of HBM per device.

v0:
```python
import math

import jax
import jax.numpy as jnp
from jax import lax
from jax.sharding import PartitionSpec as P

HEADS = 4
HEAD_DIM = 16
PATCH = 1024


EPS = 1e-05


def extended_2(block, sides, width):
    for axis, dim in sides:
        count = lax.axis_size(axis)
        forward = [(i, i + 1) for i in range(count - 1)]
        backward = [(target, source) for source, target in forward]
        low = lax.ppermute(
            lax.slice_in_dim(block, block.shape[dim] - width, None, axis=dim), axis, forward
        )
        high = lax.ppermute(lax.slice_in_dim(block, 0, width, axis=dim), axis, backward)
        block = jnp.concatenate([low, block, high], axis=dim)
    return block


def layer_norm(values, scale_gain):
    average = jnp.mean(values, axis=0, keepdims=True)
    centred = values - average
    spread = jnp.mean(centred * centred, axis=0, keepdims=True)
    return centred * lax.rsqrt(spread + EPS) * scale_gain[:, None]


def positional(extended, offsets_idx, conv_weight, scale_gain, own_cols):
    last_col = extended.shape[1] - 1
    resolved = jnp.where(offsets_idx < 0, last_col, offsets_idx)
    offsets, points = resolved.shape
    ext_rows = extended.T
    gathered = jnp.take(ext_rows, resolved.reshape(-1), axis=0).reshape(offsets, points, -1)
    convolved = jnp.einsum("opc,ocd->dp", gathered, conv_weight, preferred_element_type=jnp.float32)
    return (own_cols.astype(jnp.float32) + layer_norm(convolved, scale_gain)).astype(jnp.bfloat16)


def patch_block(patch_cols, qkv_w, out_w, up_w, down_w, gain_a, gain_b):
    channels, length = patch_cols.shape
    based = patch_cols.astype(jnp.float32)
    normed = layer_norm(based, gain_a).astype(jnp.bfloat16)
    qkv = jnp.dot(qkv_w.T, normed, preferred_element_type=jnp.float32).astype(jnp.bfloat16)
    split_qkv = qkv.reshape(3, HEADS, HEAD_DIM, length)
    scores = jnp.einsum(
        "hdq,hdk->hqk", split_qkv[0], split_qkv[1], preferred_element_type=jnp.float32
    ) * HEAD_DIM ** (-0.5)
    row_max = jnp.max(scores, axis=2, keepdims=True)
    weights = jnp.exp(scores - row_max)
    probabilities = (weights / jnp.sum(weights, axis=2, keepdims=True)).astype(jnp.bfloat16)
    mixed_out = jnp.einsum(
        "hqk,hdk->hdq", probabilities, split_qkv[2], preferred_element_type=jnp.float32
    )
    mixed_out = mixed_out.astype(jnp.bfloat16).reshape(channels, length)
    residual = based + jnp.dot(out_w.T, mixed_out, preferred_element_type=jnp.float32)
    normed_b = layer_norm(residual, gain_b).astype(jnp.bfloat16)
    hidden = jax.nn.gelu(
        jnp.dot(up_w.T, normed_b, preferred_element_type=jnp.float32), approximate=False
    )
    hidden = hidden.astype(jnp.bfloat16)
    return (residual + jnp.dot(down_w.T, hidden, preferred_element_type=jnp.float32)).astype(
        jnp.bfloat16
    )


def serial_block(layout, qkv_w, out_w, up_w, down_w, gain_a, gain_b):
    patches = layout.shape[1] // PATCH

    def advance(patch_index, outcome):
        offset_col = patch_index * PATCH
        patch_cols = lax.dynamic_slice_in_dim(layout, offset_col, PATCH, 1)
        done = patch_block(patch_cols, qkv_w, out_w, up_w, down_w, gain_a, gain_b)
        return lax.dynamic_update_slice_in_dim(outcome, done, offset_col, 1)

    return lax.fori_loop(0, patches, advance, jnp.zeros_like(layout))


def relay_rows(outgoing):
    channels = outgoing.shape[0]
    across = lax.axis_size("gx")
    down_axis = lax.axis_size("gy")
    moved = lax.all_to_all(
        outgoing.reshape(channels, across * down_axis, -1),
        ("gx", "gy"),
        split_axis=1,
        concat_axis=1,
        tiled=True,
    )
    return moved.reshape(channels, -1)


def relay_slots(slot_list):
    devices = lax.axis_size("gx") * lax.axis_size("gy")
    return lax.all_to_all(
        slot_list.reshape(devices, -1), ("gx", "gy"), split_axis=0, concat_axis=0, tiled=True
    ).reshape(-1)


def pack_places(owners, devices, capacity):
    points = owners.shape[0]
    block = math.gcd(points, 128)
    matches = (owners[None, :] == jnp.arange(devices, dtype=jnp.int32)[:, None]).astype(jnp.float32)
    grouped = matches.reshape(devices, points // block, block)
    index_row = jnp.arange(block, dtype=jnp.int32)
    strict = (index_row[:, None] < index_row[None, :]).astype(jnp.float32)
    within = jnp.einsum("dbi,ij->dbj", grouped, strict, precision=lax.Precision.HIGHEST)
    totals = jnp.sum(grouped, axis=2)
    before = jnp.cumsum(totals, axis=1) - totals
    ranking = jnp.sum(grouped * (within + before[:, :, None]), axis=0).reshape(points)
    return owners * capacity + ranking.astype(jnp.int32)


def send_out(rows, destinations, packed, devices, capacity):
    points, channels = rows.shape
    outgoing = jnp.zeros((devices * capacity, channels), rows.dtype).at[packed].set(rows)
    slot_list = jnp.full((devices * capacity,), points, jnp.int32).at[packed].set(destinations[1])
    arrived = relay_rows(outgoing.T)
    slot_in = relay_slots(slot_list)
    layout = jnp.zeros((points + 1, channels), rows.dtype).at[slot_in].set(arrived.T)
    return (layout[:points].T, slot_in)


def local(
    feats,
    face_rows,
    neighbours,
    z_dest,
    h_dest,
    conv_weight,
    qkv_weight,
    out_weight,
    up_weight,
    down_weight,
    norm_gains,
):
    channels, points = feats.shape
    devices = lax.axis_size("gx") * lax.axis_size("gy")
    capacity = 3 * points // (2 * devices)
    picked = jnp.take(feats, face_rows[0], axis=1)
    along_x = extended_2(picked[:, 0:2], (("gx", 1),), 1)
    along_y = extended_2(picked[:, 2:4], (("gy", 1),), 1)
    extended = jnp.concatenate(
        [
            feats,
            along_x[:, 0],
            along_x[:, 3],
            along_y[:, 0],
            along_y[:, 3],
            jnp.zeros((channels, 1), feats.dtype),
        ],
        axis=1,
    )
    encoded = positional(extended, neighbours, conv_weight, norm_gains[0], feats)
    z_packed = pack_places(z_dest[0], devices, capacity)
    zorder, z_slots = send_out(encoded.T, z_dest, z_packed, devices, capacity)
    first_out = serial_block(
        zorder,
        qkv_weight[0],
        out_weight[0],
        up_weight[0],
        down_weight[0],
        norm_gains[1],
        norm_gains[2],
    )
    first_rows = jnp.concatenate([first_out.T, jnp.zeros((1, channels), first_out.dtype)], axis=0)
    returned = relay_rows(jnp.take(first_rows, z_slots, axis=0).T)
    home_rows = jnp.take(returned.T, z_packed, axis=0)
    h_packed = pack_places(h_dest[0], devices, capacity)
    hilbert, _ = send_out(home_rows, h_dest, h_packed, devices, capacity)
    return serial_block(
        hilbert,
        qkv_weight[1],
        out_weight[1],
        up_weight[1],
        down_weight[1],
        norm_gains[3],
        norm_gains[4],
    )


def solution(mesh):
    placed = (
        P(None, ("gx", "gy")),
        P(("gx", "gy"), None, None),
        P(None, ("gx", "gy")),
        P(None, ("gx", "gy")),
        P(None, ("gx", "gy")),
        P(),
        P(),
        P(),
        P(),
        P(),
        P(),
    )
    return jax.shard_map(
        local, mesh=mesh, in_specs=placed, out_specs=P(None, ("gx", "gy")), check_vma=False
    )
```

profile of v0, /device:TPU:1, one launch (start us, length us, event | category | flops | bytes accessed | tf_op | source)
XLA Modules:
  0.0 931.1 jit_solution(6885115123862926733)
XLA Ops:
  18.0 15.5 %scatter_custom_fusion.1 = s32[6144]{0:T(1024)S(1)} fusion(s32[4096]{0:T(1024)S(1)} %bitcast.421, s32[4096]{0:T(1024)S(1)} %bitcast.437, s32[]{:T(128)} %constant.561.clone.1), kind=kCustom, calls=%fused_computation.327 | custom fusion | bytes 24580 | tf_op jit(solution)/shard_map/scatter | solution.py:123
  34.3 12.0 %all-to-all-start.1 = ((s32[128,1,48]{2,1,0:T(1,128)}), s32[128,1,48]{2,1,0:T(1,128)S(1)}, u32[]{:S(2)}, u32[]{:S(2)}) async-start(s32[128,1,48]{2,1,0:T(1,128)} %bitcast.37), calls=%async_computation.1 | async-start | bytes 131072 | tf_op jit(solution)/shard_map/all_to_all | solution.py:101
  52.2 15.5 %scatter_custom_fusion = s32[6144]{0:T(1024)S(1)} fusion(s32[4096]{0:T(1024)S(1)} %bitcast.435, s32[4096]{0:T(1024)S(1)} %bitcast.438, s32[]{:T(128)} %constant.561.clone.1), kind=kCustom, calls=%fused_computation.329 | custom fusion | bytes 24580 | tf_op jit(solution)/shard_map/scatter | solution.py:123
  68.6 383.1 %gather_fusion.1 = bf16[110592,64]{1,0:T(8,128)(2,1)} fusion(bf16[4609,64]{1,0:T(8,128)(2,1)S(1)} %bitcast.393, s32[110592]{0:T(1024)S(1)} %broadcast_clamp_fusion), kind=kCustom, calls=%fused_computation.1 | custom fusion | bytes 28753920 | tf_op jit(solution)/shard_map/jit(_take)/gather | solution.py:41
  451.7 26.1 %copy.42 = bf16[27,4096,64]{1,2,0:T(8,128)(2,1)} copy(bf16[27,4096,64]{2,1,0:T(8,128)(2,1)} %bitcast.394) | data formatting | bytes 28311552 | tf_op jit(solution)/shard_map/jit(_take)/gather | solution.py:41
  485.3 11.5 %scatter_custom_fusion.2 = bf16[6144,64]{1,0:T(8,128)(2,1)S(1)} fusion(s32[4096]{0:T(1024)S(1)} %bitcast.422, bf16[4096,64]{1,0:T(8,128)(2,1)S(1)} %copy.44, bf16[]{:T(256)} %constant.560.clone.1), kind=kCustom, calls=%fused_computation.288 | custom fusion | bytes 786434 | tf_op jit(solution)/shard_map/scatter | solution.py:122
  511.1 14.0 %all-to-all-done.2 = bf16[128,2,1536]{2,1,0:T(2,128)(2,1)S(1)} async-done(((bf16[128,2,1536]{2,1,0:T(2,128)(2,1)}), bf16[128,2,1536]{2,1,0:T(2,128)(2,1)S(1)}, u32[]{:S(2)}, u32[]{:S(2)}) %all-to-all-start.2) | async-done | bytes 786464 | tf_op jit(solution)/shard_map/all_to_all | solution.py:89
  531.2 16.2 %scatter_custom_fusion.3 = bf16[4097,64]{1,0:T(8,128)(2,1)S(1)} fusion(s32[6144]{0:T(1024)S(1)} %bitcast.419, bf16[6144,64]{1,0:T(8,128)(2,1)S(1)} %bitcast.414, bf16[]{:T(256)} %constant.560.clone.1), kind=kCustom, calls=%fused_computation.292 | custom fusion | bytes 524418 | tf_op jit(solution)/shard_map/scatter | solution.py:126
  547.9 127.2 %while.26 = (s32[]{:T(128)}, bf16[64,4096]{1,0:T(8,128)(2,1)S(1)}, bf16[64,4096]{1,0:T(8,128)(2,1)S(1)}, f32[1,64]{1,0:T(1,128)S(1)}, bf16[64,192]{1,0:T(8,128)(...) while((s32[]{:T(128)}, bf16[64,4096]{1,0:T(8,128)(2,1)S(1)}, ...), condition=%wide.region_19.20_spmd, body=%wide.region_12.0_spmd.sunk | while | flops 555687936 | bytes 37602496 | solution.py:82
  561.7 14.9 %fusion.365 = bf16[4,16,1024]{2,1,0:T(8,128)(2,1)S(1)} fusion(bf16[4,16,1024]{2,1,0:T(8,128)(2,1)S(1)} %bitcast.410, f32[4,1024]{1,0:T(4,128)S(1)} %fusion.363, f32[4,1024,1024]{1,2,0:T(8,128)} %fusion.364), kind=kOutput, calls=%fused_computation.26.clone.1 | convolution fusion | flops 155259904 | bytes 17055744 | tf_op jit(solution)/shard_map/while/body/eval_jaxpr/hqk,hdk->hdq/dot_general | solution.py:58
  593.5 14.9 %fusion.365 = bf16[4,16,1024]{2,1,0:T(8,128)(2,1)S(1)} fusion(bf16[4,16,1024]{2,1,0:T(8,128)(2,1)S(1)} %bitcast.410, f32[4,1024]{1,0:T(4,128)S(1)} %fusion.363, f32[4,1024,1024]{1,2,0:T(8,128)} %fusion.364), kind=kOutput, calls=%fused_computation.26.clone.1 | convolution fusion | flops 155259904 | bytes 17055744 | tf_op jit(solution)/shard_map/while/body/eval_jaxpr/hqk,hdk->hdq/dot_general | solution.py:58
  625.3 14.9 %fusion.365 = bf16[4,16,1024]{2,1,0:T(8,128)(2,1)S(1)} fusion(bf16[4,16,1024]{2,1,0:T(8,128)(2,1)S(1)} %bitcast.410, f32[4,1024]{1,0:T(4,128)S(1)} %fusion.363, f32[4,1024,1024]{1,2,0:T(8,128)} %fusion.364), kind=kOutput, calls=%fused_computation.26.clone.1 | convolution fusion | flops 155259904 | bytes 17055744 | tf_op jit(solution)/shard_map/while/body/eval_jaxpr/hqk,hdk->hdq/dot_general | solution.py:58
  657.1 14.9 %fusion.365 = bf16[4,16,1024]{2,1,0:T(8,128)(2,1)S(1)} fusion(bf16[4,16,1024]{2,1,0:T(8,128)(2,1)S(1)} %bitcast.410, f32[4,1024]{1,0:T(4,128)S(1)} %fusion.363, f32[4,1024,1024]{1,2,0:T(8,128)} %fusion.364), kind=kOutput, calls=%fused_computation.26.clone.1 | convolution fusion | flops 155259904 | bytes 17055744 | tf_op jit(solution)/shard_map/while/body/eval_jaxpr/hqk,hdk->hdq/dot_general | solution.py:58
  675.9 22.1 %gather_fusion.2 = bf16[6144,64]{1,0:T(8,128)(2,1)} fusion(bf16[4097,64]{1,0:T(8,128)(2,1)S(1)} %concatenate.7, s32[6144]{0:T(1024)S(1)} %copy-done.8), kind=kCustom, calls=%fused_computation.2 | custom fusion | bytes 1597440 | tf_op jit(solution)/shard_map/jit(_take)/gather | solution.py:173
  704.5 9.9 %all-to-all-start.3 = ((bf16[128,2,1536]{2,1,0:T(2,128)(2,1)}), bf16[128,2,1536]{2,1,0:T(2,128)(2,1)S(1)}, u32[]{:S(2)}, u32[]{:S(2)}) async-start(bf16[128,2,1536]{2,1,0:T(2,128)(2,1)} %reshape.562), calls=%async_computation.3 | async-start | bytes 1572864 | tf_op jit(solution)/shard_map/all_to_all | solution.py:89
  716.3 14.8 %all-to-all-done.3 = bf16[128,2,1536]{2,1,0:T(2,128)(2,1)S(1)} async-done(((bf16[128,2,1536]{2,1,0:T(2,128)(2,1)}), bf16[128,2,1536]{2,1,0:T(2,128)(2,1)S(1)}, u32[]{:S(2)}, u32[]{:S(2)}) %all-to-all-start.3) | async-done | bytes 786464 | tf_op jit(solution)/shard_map/all_to_all | solution.py:89
  732.1 26.9 %scatter_custom_fusion.4 = bf16[6144,64]{1,0:T(8,128)(2,1)} fusion(s32[4096]{0:T(1024)} %bitcast.436, pred[4096]{0:T(1024)(128)(4,1)S(1)} %compare_and_fusion.2, bf16[]{:T(256)} %constant.560.clone.1, bf16[]{:T(256)} %constant.570.clone.1, bf16[6144,64]{1,0:T(8,128)(2,1)S(1)} %bitcast.403, s32[4096]{0:T(1024)S(1)} %broadcast_clamp_fusion.2), kind=kCustom, calls=%fused_computation.281 | custom fusion | flops 262144 | bytes 1594368 | tf_op jit(solution)/shard_map/scatter | solution.py:122
  766.9 16.8 %all-to-all-done.4 = bf16[128,2,1536]{2,1,0:T(2,128)(2,1)S(1)} async-done(((bf16[128,2,1536]{2,1,0:T(2,128)(2,1)}), bf16[128,2,1536]{2,1,0:T(2,128)(2,1)S(1)}, u32[]{:S(2)}, u32[]{:S(2)}) %all-to-all-start.4) | async-done | bytes 786464 | tf_op jit(solution)/shard_map/all_to_all | solution.py:89
  784.7 16.2 %scatter_custom_fusion.5 = bf16[4097,64]{1,0:T(8,128)(2,1)S(1)} fusion(s32[6144]{0:T(1024)S(1)} %bitcast.432, bf16[6144,64]{1,0:T(8,128)(2,1)S(1)} %bitcast.415, bf16[]{:T(256)} %constant.560.clone.1), kind=kCustom, calls=%fused_computation.290 | custom fusion | bytes 524418 | tf_op jit(solution)/shard_map/scatter | solution.py:126
  801.7 127.4 %while.27 = (s32[]{:T(128)}, bf16[64,4096]{1,0:T(8,128)(2,1)S(1)}, bf16[64,4096]{1,0:T(8,128)(2,1)S(1)}, f32[1,64]{1,0:T(1,128)S(1)}, bf16[64,192]{1,0:T(8,128)(...) while((s32[]{:T(128)}, bf16[64,4096]{1,0:T(8,128)(2,1)S(1)}, ...), condition=%wide.region_29.30_spmd, body=%wide.region_22.29_spmd.sunk | while | flops 555687936 | bytes 37602496 | solution.py:82
  815.7 14.9 %fusion.385 = bf16[4,16,1024]{2,1,0:T(8,128)(2,1)S(1)} fusion(bf16[4,16,1024]{2,1,0:T(8,128)(2,1)S(1)} %bitcast.411, f32[4,1024]{1,0:T(4,128)S(1)} %fusion.383, f32[4,1024,1024]{1,2,0:T(8,128)} %fusion.384), kind=kOutput, calls=%fused_computation.151.clone.1 | convolution fusion | flops 155259904 | bytes 17055744 | tf_op jit(solution)/shard_map/while/body/eval_jaxpr/hqk,hdk->hdq/dot_general | solution.py:58
  847.5 14.9 %fusion.385 = bf16[4,16,1024]{2,1,0:T(8,128)(2,1)S(1)} fusion(bf16[4,16,1024]{2,1,0:T(8,128)(2,1)S(1)} %bitcast.411, f32[4,1024]{1,0:T(4,128)S(1)} %fusion.383, f32[4,1024,1024]{1,2,0:T(8,128)} %fusion.384), kind=kOutput, calls=%fused_computation.151.clone.1 | convolution fusion | flops 155259904 | bytes 17055744 | tf_op jit(solution)/shard_map/while/body/eval_jaxpr/hqk,hdk->hdq/dot_general | solution.py:58
  879.3 14.9 %fusion.385 = bf16[4,16,1024]{2,1,0:T(8,128)(2,1)S(1)} fusion(bf16[4,16,1024]{2,1,0:T(8,128)(2,1)S(1)} %bitcast.411, f32[4,1024]{1,0:T(4,128)S(1)} %fusion.383, f32[4,1024,1024]{1,2,0:T(8,128)} %fusion.384), kind=kOutput, calls=%fused_computation.151.clone.1 | convolution fusion | flops 155259904 | bytes 17055744 | tf_op jit(solution)/shard_map/while/body/eval_jaxpr/hqk,hdk->hdq/dot_general | solution.py:58
  911.1 14.9 %fusion.385 = bf16[4,16,1024]{2,1,0:T(8,128)(2,1)S(1)} fusion(bf16[4,16,1024]{2,1,0:T(8,128)(2,1)S(1)} %bitcast.411, f32[4,1024]{1,0:T(4,128)S(1)} %fusion.383, f32[4,1024,1024]{1,2,0:T(8,128)} %fusion.384), kind=kOutput, calls=%fused_computation.151.clone.1 | convolution fusion | flops 155259904 | bytes 17055744 | tf_op jit(solution)/shard_map/while/body/eval_jaxpr/hqk,hdk->hdq/dot_general | solution.py:58
  (243 shorter events, 209.0 us)
Async XLA Ops:
  0.0 477.9 %copy-start = (bf16[27,64,64]{2,1,0:T(8,128)(2,1)S(1)}, bf16[27,64,64]{2,1,0:T(8,128)(2,1)}, u32[]{:S(2)}) copy-start(bf16[27,64,64]{2,1,0:T(8,128)(2,1)} %param.20) | copy-start | bytes 663556
  0.0 16.1 %copy-start.9 = (s32[2,4096]{1,0:T(2,128)S(1)}, s32[2,4096]{1,0:T(2,128)}, u32[]{:S(2)}) copy-start(s32[2,4096]{1,0:T(2,128)} %param.18) | copy-start | bytes 98308
  5.1 63.4 %collective-permute-start = (bf16[64,1,128]{0,2,1:T(8,128)(2,1)}, bf16[64,1,128]{0,2,1:T(8,128)(2,1)S(1)}, u32[]{:S(2)}, u32[]{:S(2)}) collective-permute-start(bf16[64,1,128]{0,2,1:T(8,128)(2,1)} %get-tuple-element.418), channel_id=1, source_target_pairs={{0,16},{16,32},{32,48},{48,64},{64,80},{80,96},{96,112},{1,17},{17... | collective-permute-start | bytes 49160 | tf_op jit(solution)/shard_map/ppermute | solution.py:21
  9.6 58.9 %collective-permute-start.1 = (bf16[64,1,128]{0,2,1:T(8,128)(2,1)}, bf16[64,1,128]{0,2,1:T(8,128)(2,1)S(1)}, u32[]{:S(2)}, u32[]{:S(2)}) collective-permute-start(bf16[64,1,128]{0,2,1:T(8,128)(2,1)} %get-tuple-element.417), channel_id=1, source_target_pairs={{16,0},{32,16},{48,32},{64,48},{80,64},{96,80},{112,96},{17,1},{33... | collective-permute-start | bytes 49160 | tf_op jit(solution)/shard_map/ppermute | solution.py:24
  11.6 57.0 %collective-permute-start.2 = (bf16[64,1,128]{0,2,1:T(8,128)(2,1)}, bf16[64,1,128]{0,2,1:T(8,128)(2,1)S(1)}, u32[]{:S(2)}, u32[]{:S(2)}) collective-permute-start(bf16[64,1,128]{0,2,1:T(8,128)(2,1)} %get-tuple-element.416), channel_id=1, source_target_pairs={{0,1},{1,2},{2,3},{3,4},{4,5},{5,6},{6,7},{7,8},{8,9},{9,10},{10,1... | collective-permute-start | bytes 49160 | tf_op jit(solution)/shard_map/ppermute | solution.py:21
  14.8 53.8 %collective-permute-start.3 = (bf16[64,1,128]{0,2,1:T(8,128)(2,1)S(1)}, bf16[64,1,128]{0,2,1:T(8,128)(2,1)S(1)}, u32[]{:S(2)}, u32[]{:S(2)}) collective-permute-start(bf16[64,1,128]{0,2,1:T(8,128)(2,1)S(1)} %get-tuple-element.415), channel_id=1, source_target_pairs={{1,0},{2,1},{3,2},{4,3},{5,4},{6,5},{7,6},{8,7},{9,8},{10,9},{11,1... | collective-permute-start | bytes 49160 | tf_op jit(solution)/shard_map/ppermute | solution.py:24
  17.2 29.2 %copy-start.3 = (s32[27,4096]{1,0:T(8,128)S(1)}, s32[27,4096]{1,0:T(8,128)}, u32[]{:S(2)}) copy-start(s32[27,4096]{1,0:T(8,128)} %param.17) | copy-start | bytes 1327108
  18.0 16.3 %copy-start.17 = (f32[32,128]{1,0:T(8,128)}, f32[32,128]{1,0:T(8,128)S(1)}, u32[]{:S(2)}) copy-start(f32[32,128]{1,0:T(8,128)S(1)} %select_reduce_fusion) | copy-start | bytes 49156
  18.0 467.3 %copy-start.12 = (s32[4096,1]{0,1:T(1,128)}, s32[4096,1]{0,1:T(1,128)S(1)}, u32[]{:S(2)}) copy-start(s32[4096,1]{0,1:T(1,128)S(1)} %compare_select_fusion.5) | copy-start | bytes 49156
  34.3 464.3 %all-to-all-start.1 = ((s32[128,1,48]{2,1,0:T(1,128)}), s32[128,1,48]{2,1,0:T(1,128)S(1)}, u32[]{:S(2)}, u32[]{:S(2)}) async-start(s32[128,1,48]{2,1,0:T(1,128)} %bitcast.37), calls=%async_computation.1 | async-start | bytes 131072 | tf_op jit(solution)/shard_map/all_to_all | solution.py:101
  46.5 3.1 copy-start.19
  46.5 3.7 copy-start.10
  47.7 3.8 copy-start.24
  51.5 400.2 %copy-start.23 = (s32[4096,1]{0,1:T(1,128)}, s32[4096,1]{0,1:T(1,128)S(1)}, u32[]{:S(2)}) copy-start(s32[4096,1]{0,1:T(1,128)S(1)} %compare_select_fusion.6) | copy-start | bytes 49156
  477.9 6.7 copy-start.2
  498.6 26.4 %all-to-all-start.2 = ((bf16[128,2,1536]{2,1,0:T(2,128)(2,1)}), bf16[128,2,1536]{2,1,0:T(2,128)(2,1)S(1)}, u32[]{:S(2)}, u32[]{:S(2)}) async-start(bf16[128,2,1536]{2,1,0:T(2,128)(2,1)} %reshape.560), calls=%async_computation.2 | async-start | bytes 1572864 | tf_op jit(solution)/shard_map/all_to_all | solution.py:89
  525.1 179.5 %all-to-all-start = ((s32[128,1,48]{2,1,0:T(1,128)}), s32[128,1,48]{2,1,0:T(1,128)}, u32[]{:S(2)}, u32[]{:S(2)}) async-start(s32[128,1,48]{2,1,0:T(1,128)} %bitcast.28), calls=%async_computation | async-start | bytes 131072 | tf_op jit(solution)/shard_map/all_to_all | solution.py:101
  675.9 22.1 %copy-start.21 = (pred[6144]{0:T(1024)(128)(4,1)S(1)}, pred[6144]{0:T(1024)(128)(4,1)}, u32[]{:S(2)}) copy-start(pred[6144]{0:T(1024)(128)(4,1)} %compare_and_fusion.1) | copy-start | bytes 18436
  702.3 12.1 %copy-start.7 = (bf16[1,256,64]{1,2,0:T(8,128)(2,1)S(1)}, bf16[1,256,64]{1,2,0:T(8,128)(2,1)}, u32[]{:S(2)}) copy-start(bf16[1,256,64]{1,2,0:T(8,128)(2,1)} %get-tuple-element.419) | copy-start | bytes 98308
  702.3 12.2 %copy-start.13 = (s32[4096,1]{0,1:T(1,128)S(1)}, s32[4096,1]{0,1:T(1,128)}, u32[]{:S(2)}) copy-start(s32[4096,1]{0,1:T(1,128)} %copy-done.12) | copy-start | bytes 49156
  702.3 12.2 %copy-start.11 = (s32[1,4096]{1,0:T(1,128)S(1)}, s32[1,4096]{1,0:T(1,128)}, u32[]{:S(2)}) copy-start(s32[1,4096]{1,0:T(1,128)} %get-tuple-element.428) | copy-start | bytes 49156
  702.3 12.2 %copy-start.18 = (f32[32,128]{1,0:T(8,128)S(1)}, f32[32,128]{1,0:T(8,128)}, u32[]{:S(2)}) copy-start(f32[32,128]{1,0:T(8,128)} %copy-done.17) | copy-start | bytes 49156
  704.5 26.6 %all-to-all-start.3 = ((bf16[128,2,1536]{2,1,0:T(2,128)(2,1)}), bf16[128,2,1536]{2,1,0:T(2,128)(2,1)S(1)}, u32[]{:S(2)}, u32[]{:S(2)}) async-start(bf16[128,2,1536]{2,1,0:T(2,128)(2,1)} %reshape.562), calls=%async_computation.3 | async-start | bytes 1572864 | tf_op jit(solution)/shard_map/all_to_all | solution.py:89
  762.7 21.0 %all-to-all-start.4 = ((bf16[128,2,1536]{2,1,0:T(2,128)(2,1)}), bf16[128,2,1536]{2,1,0:T(2,128)(2,1)S(1)}, u32[]{:S(2)}, u32[]{:S(2)}) async-start(bf16[128,2,1536]{2,1,0:T(2,128)(2,1)} %reshape.564), calls=%async_computation.4 | async-start | bytes 1572864 | tf_op jit(solution)/shard_map/all_to_all | solution.py:89
  (11 other events, 12.2 us)
where the time goes:
time: 941 us; the launch traced here: 931 us
  local copies, waits for them, and re-layouts  531 us (56%)
  matrix products  260 us (28%)
  starting transfers between devices  51.8 us (6%)
  waiting for transfers between devices  45.5 us (5%)
  other arithmetic  40.3 us (4%)
    gather x2, local copies, waits for them, and re-layouts, positional(): jnp.take(ext_rows, resolved.reshape(-1), axis=0)  409 us
    dot_general x8, matrix products, patch_block(): jnp.einsum('hqk,hdk->hdq', probabilities, split_qkv[2], preferred_element...  120 us
    dot_general x8, matrix products, patch_block(): jnp.einsum('hdq,hdk->hqk', split_qkv[0], split_qkv[1], preferred_element_...  64.7 us
    all_to_all x3, waiting for transfers between devices, relay_rows(): lax.all_to_all(outgoing.reshape(channels, across * down_axis, -1), ('gx',...  45.5 us
    sub x8, matrix products, patch_block(): weights = jnp.exp(scores - row_max)  41.5 us
    scatter x2, local copies, waits for them, and re-layouts, send_out(): jnp.zeros((points + 1, channels), rows.dtype).at[slot_in].set(arrived.T)  32.5 us
    scatter x2, local copies, waits for them, and re-layouts, send_out(): jnp.full((devices * capacity,), points, jnp.int32).at[packed]  31.1 us
    scatter x1, other arithmetic, send_out(): jnp.zeros((devices * capacity, channels), rows.dtype).at[packed].set(rows)  26.9 us
  transfers between devices with their start and end apart: 9, of which 3 were waited for; matrix products, arithmetic and copies ran while one was open for 69% of the time, Pallas kernels for 0%

commit v1 on v0

v1 whole, which is shorter than its diff:
```python
import functools

import jax
import jax.numpy as jnp
from jax import lax
from jax.experimental import pallas as pl
from jax.experimental.pallas import tpu as pltpu
from jax.sharding import PartitionSpec as P

HEADS = 4
HEAD_DIM = 16
PATCH = 1024
C = 64
PTS = 4096
FACE = 128
EXT = PTS + 4 * FACE
TROWS = EXT + 8
DEV = 128
CAP = 48
HALF = CAP // 2
PACK = DEV * HALF
PAIRS = 13
BLK = 512
UN = 8
EPS = 1e-05
VMEM = 60 * 2**20
BF = jnp.bfloat16
F32 = jnp.float32


def lane_norm(values, gain):
    average = jnp.mean(values, axis=1, keepdims=True)
    centred = values - average
    spread = jnp.mean(centred * centred, axis=1, keepdims=True)
    return centred * lax.rsqrt(spread + EPS) * gain


def chan_norm(values, gain):
    average = jnp.mean(values, axis=0, keepdims=True)
    centred = values - average
    spread = jnp.mean(centred * centred, axis=0, keepdims=True)
    return centred * lax.rsqrt(spread + EPS) * gain


def low_lanes(rows):
    return lax.broadcasted_iota(jnp.int32, (rows, 128), 1) < C


def pack_rows(rows_ref, out_ref):
    def part(b, _):
        at = pl.multiple_of(b * 512, 512)
        low = rows_ref[pl.ds(at, 512), :]
        high = pltpu.roll(rows_ref[pl.ds(at + PACK, 512), :], C, 1)
        out_ref[pl.ds(at, 512), :] = jnp.where(low_lanes(512), low, high).astype(BF)
        return 0

    lax.fori_loop(0, PACK // 512, part, 0)


def unpack_rows(in_ref, rows_ref):
    def part(b, _):
        at = pl.multiple_of(b * 512, 512)
        both = in_ref[pl.ds(at, 512), :].astype(F32)
        rows_ref[pl.ds(at, 512), :] = both
        rows_ref[pl.ds(at + PACK, 512), :] = pltpu.roll(both, C, 1)
        return 0

    lax.fori_loop(0, PACK // 512, part, 0)


def conv_kernel(idx_ref, place_ref, ext_ref, pair_ref, self_ref, gain_ref, out_ref, table, sums, rows):
    step = pl.program_id(0)

    @pl.when(step == 0)
    def _():
        def fill(b, _):
            at = pl.multiple_of(b * 512, 512)
            chunk = ext_ref[pl.ds(at, 512), :]
            for j in range(PAIRS):
                table[pl.ds(pl.multiple_of(j * TROWS + at, 8), 512), :] = jnp.dot(
                    chunk, pair_ref[j], preferred_element_type=F32
                )
            return 0

        lax.fori_loop(0, EXT // 512, fill, 0)
        for j in range(PAIRS):
            table[j * TROWS + EXT : (j + 1) * TROWS, :] = jnp.zeros((TROWS - EXT, 128), F32)

    low_row = low_lanes(1)

    def gather(g, _):
        for u in range(UN):
            i = g * UN + u
            even, odd = None, None
            for j in range(PAIRS):
                a = table[pl.ds(idx_ref[2 * j, i], 1), :]
                b = table[pl.ds(idx_ref[2 * j + 1, i], 1), :]
                even = a if even is None else even + a
                odd = b if odd is None else odd + b
            sums[pl.ds(i, 1), :] = jnp.where(low_row, even, odd)
        return 0

    lax.fori_loop(0, BLK // UN, gather, 0)
    own = ext_ref[pl.ds(pl.multiple_of(step * BLK, BLK), BLK), :]
    both = sums[...]
    conv = both[:, :C] + both[:, C:] + jnp.dot(own, self_ref[...], preferred_element_type=F32)
    encoded = own.astype(F32) + lane_norm(conv, gain_ref[...])
    sums[:, :C] = encoded

    def scatter(g, _):
        for u in range(UN):
            i = g * UN + u
            rows[pl.ds(place_ref[step * BLK + i], 1), :] = sums[pl.ds(i, 1), :]
        return 0

    lax.fori_loop(0, BLK // UN, scatter, 0)

    @pl.when(step == pl.num_programs(0) - 1)
    def _():
        pack_rows(rows, out_ref)


def conv_send(idx, place, ext_rows, pair_w, self_w, gain):
    steps = PTS // BLK
    return pl.pallas_call(
        conv_kernel,
        grid=(steps,),
        in_specs=[
            pl.BlockSpec((2 * PAIRS, BLK), lambda s: (0, s), memory_space=pltpu.SMEM),
            pl.BlockSpec(memory_space=pltpu.SMEM),
            pl.BlockSpec((EXT, C), lambda s: (0, 0)),
            pl.BlockSpec((PAIRS, C, 128), lambda s: (0, 0, 0)),
            pl.BlockSpec((C, C), lambda s: (0, 0)),
            pl.BlockSpec((1, C), lambda s: (0, 0)),
        ],
        out_specs=pl.BlockSpec((PACK, 128), lambda s: (0, 0)),
        out_shape=jax.ShapeDtypeStruct((PACK, 128), BF),
        scratch_shapes=[
            pltpu.VMEM((PAIRS * TROWS, 128), F32),
            pltpu.VMEM((BLK, 128), F32),
            pltpu.VMEM((2 * PACK, 128), F32),
        ],
        compiler_params=pltpu.CompilerParams(vmem_limit_bytes=VMEM),
        cost_estimate=pl.CostEstimate(flops=10**11, bytes_accessed=10**6, transcendentals=0),
        name="conv_send",
    )(idx, place, ext_rows, pair_w, self_w, gain)


def relay_kernel(from_ref, to_ref, in_ref, out_ref, source, target):
    unpack_rows(in_ref, source)

    def move(g, _):
        for u in range(UN):
            i = g * UN + u
            target[pl.ds(to_ref[i], 1), :] = source[pl.ds(from_ref[i], 1), :]
        return 0

    lax.fori_loop(0, PTS // UN, move, 0)
    pack_rows(target, out_ref)


def relay(place_from, place_to, packed):
    return pl.pallas_call(
        relay_kernel,
        in_specs=[
            pl.BlockSpec(memory_space=pltpu.SMEM),
            pl.BlockSpec(memory_space=pltpu.SMEM),
            pl.BlockSpec(memory_space=pltpu.VMEM),
        ],
        out_specs=pl.BlockSpec(memory_space=pltpu.VMEM),
        out_shape=jax.ShapeDtypeStruct((PACK, 128), BF),
        scratch_shapes=[
            pltpu.VMEM((2 * PACK, 128), F32),
            pltpu.VMEM((2 * PACK, 128), F32),
        ],
        compiler_params=pltpu.CompilerParams(vmem_limit_bytes=VMEM),
        cost_estimate=pl.CostEstimate(flops=10**9, bytes_accessed=10**6, transcendentals=0),
        name="relay",
    )(place_from, place_to, packed)


def patch_math(x, qkv_ref, outw_ref, up_ref, down_ref, gain_a_ref, gain_b_ref, mixed):
    normed = chan_norm(x, gain_a_ref[...]).astype(BF)
    qkv = jnp.dot(qkv_ref[...], normed, preferred_element_type=F32).astype(BF)
    queries = qkv[:C].astype(F32) * HEAD_DIM**-0.5
    keys = qkv[C : 2 * C].astype(F32).T.astype(BF)
    head_of = lax.broadcasted_iota(jnp.int32, (C, PATCH), 0) // HEAD_DIM
    ones = jnp.ones((HEAD_DIM, PATCH), BF)
    for h in range(HEADS):
        masked = jnp.where(head_of == h, queries, 0.0).astype(BF)
        scores = jnp.dot(keys, masked, preferred_element_type=F32)
        weights = jnp.exp(scores - jnp.max(scores, axis=0, keepdims=True)).astype(BF)
        first = 2 * C + h * HEAD_DIM
        values = jnp.concatenate([qkv[first : first + HEAD_DIM], ones], axis=0)
        summed = jnp.dot(values, weights, preferred_element_type=F32)
        mixed[h * HEAD_DIM : (h + 1) * HEAD_DIM, :] = (
            summed[:HEAD_DIM] / summed[HEAD_DIM : HEAD_DIM + 1]
        ).astype(BF)
    residual = x + jnp.dot(outw_ref[...], mixed[...], preferred_element_type=F32)
    normed_b = chan_norm(residual, gain_b_ref[...]).astype(BF)
    raised = jnp.dot(up_ref[...], normed_b, preferred_element_type=F32)
    hidden = (0.5 * raised * (1.0 + lax.erf(raised * 0.5**0.5))).astype(BF)
    return residual + jnp.dot(down_ref[...], hidden, preferred_element_type=F32)


def block_kernel(
    back, slot_ref, in_ref, qkv_ref, outw_ref, up_ref, down_ref, ga_ref, gb_ref, out_ref,
    source, rows, mixed,
):
    unpack_rows(in_ref, source)

    def place(g, _):
        for u in range(UN):
            i = g * UN + u
            rows[pl.ds(slot_ref[i], 1), :] = source[pl.ds(i, 1), :]
        return 0

    lax.fori_loop(0, 2 * PACK // UN, place, 0)

    def patch(p, _):
        at = pl.multiple_of(p * PATCH, PATCH)
        x = rows[pl.ds(at, PATCH), :].T[:C]
        y = patch_math(x, qkv_ref, outw_ref, up_ref, down_ref, ga_ref, gb_ref, mixed)
        if back:
            rows[pl.ds(at, PATCH), :] = jnp.concatenate([y, y], axis=0).T
        else:
            out_ref[:, pl.ds(at, PATCH)] = y.astype(BF)
        return 0

    lax.fori_loop(0, PTS // PATCH, patch, 0)
    if back:
        low_row = low_lanes(1)

        def fetch(g, _):
            for u in range(UN):
                i = g * UN + u
                low = rows[pl.ds(slot_ref[i], 1), :]
                high = rows[pl.ds(slot_ref[i + PACK], 1), :]
                source[pl.ds(i, 1), :] = jnp.where(low_row, low, high)
            return 0

        lax.fori_loop(0, PACK // UN, fetch, 0)
        out_ref[...] = source[0:PACK, :].astype(BF)


def block(back, slots, packed, qkv_w, out_w, up_w, down_w, gain_a, gain_b):
    out = (PACK, 128) if back else (C, PTS)
    return pl.pallas_call(
        functools.partial(block_kernel, back),
        in_specs=[pl.BlockSpec(memory_space=pltpu.SMEM)]
        + [pl.BlockSpec(memory_space=pltpu.VMEM)] * 7,
        out_specs=pl.BlockSpec(memory_space=pltpu.VMEM),
        out_shape=jax.ShapeDtypeStruct(out, BF),
        scratch_shapes=[
            pltpu.VMEM((2 * PACK, 128), F32),
            pltpu.VMEM((PTS + 8, 128), F32),
            pltpu.VMEM((C, PATCH), BF),
        ],
        compiler_params=pltpu.CompilerParams(vmem_limit_bytes=VMEM),
        cost_estimate=pl.CostEstimate(flops=4 * 10**10, bytes_accessed=10**6, transcendentals=0),
        name="block_back" if back else "block_last",
    )(slots, packed, qkv_w.T, out_w.T, up_w.T, down_w.T, gain_a[:, None], gain_b[:, None])


def beside(block_cols, sides, width):
    for axis, dim in sides:
        count = lax.axis_size(axis)
        forward = [(i, i + 1) for i in range(count - 1)]
        backward = [(target, source) for source, target in forward]
        low = lax.ppermute(block_cols[:, 1], axis, forward)
        high = lax.ppermute(block_cols[:, 0], axis, backward)
    return low, high


def places(dest):
    owners, slots = dest[0], dest[1]
    lanes = 128
    matches = (owners[None, :] == jnp.arange(DEV, dtype=jnp.int32)[:, None]).astype(BF)
    grouped = matches.reshape(DEV, PTS // lanes, lanes)
    index_row = jnp.arange(lanes, dtype=jnp.int32)
    strict = (index_row[:, None] < index_row[None, :]).astype(BF)
    within = jnp.einsum("dbi,ij->dbj", grouped, strict, preferred_element_type=F32)
    totals = jnp.sum(grouped.astype(F32), axis=2)
    before = jnp.cumsum(totals, axis=1) - totals
    ranking = jnp.sum(grouped.astype(F32) * (within + before[:, :, None]), axis=0)
    ranking = ranking.reshape(PTS).astype(jnp.int32)
    place = (ranking // HALF) * PACK + owners * HALF + ranking % HALF
    ranks = (ranking[:, None] == jnp.arange(CAP, dtype=jnp.int32)[None, :]).astype(BF)
    coded = slots + 1
    high = ranks * (coded // 64).astype(BF)[:, None]
    low = ranks * (coded % 64).astype(BF)[:, None]
    listed = jnp.dot(
        matches, jnp.concatenate([high, low], axis=1), preferred_element_type=F32
    ).astype(jnp.int32)
    listed = listed[:, :CAP] * 64 + listed[:, CAP:]
    return place, jnp.where(listed == 0, PTS, listed - 1)


def exchange(packed):
    shaped = packed.reshape(DEV, HALF, 128)
    moved = lax.all_to_all(shaped, ("gx", "gy"), split_axis=0, concat_axis=0, tiled=True)
    return moved.reshape(PACK, 128)


def local(
    feats,
    face_rows,
    neighbours,
    z_dest,
    h_dest,
    conv_weight,
    qkv_weight,
    out_weight,
    up_weight,
    down_weight,
    norm_gains,
):
    picked = jnp.take(feats, face_rows[0], axis=1)
    low_x, high_x = beside(picked[:, 0:2], (("gx", 1),), 1)
    low_y, high_y = beside(picked[:, 2:4], (("gy", 1),), 1)
    ext_rows = jnp.concatenate([feats, low_x, high_x, low_y, high_y], axis=1).T

    z_place, z_list = places(z_dest)
    h_place, h_list = places(h_dest)
    slots = lax.all_to_all(
        jnp.concatenate([z_list, h_list], axis=1), ("gx", "gy"),
        split_axis=0, concat_axis=0, tiled=True,
    )
    slots = slots.reshape(DEV, 4, HALF).transpose(1, 0, 2).reshape(2, 2 * PACK)

    others = jnp.concatenate([neighbours[:PAIRS], neighbours[PAIRS + 1 :]], axis=0)
    base = (jnp.arange(2 * PAIRS, dtype=jnp.int32) // 2 * TROWS)[:, None]
    idx = jnp.where(others < 0, EXT, others) + base
    pair_w = jnp.concatenate([conv_weight[:PAIRS], conv_weight[PAIRS + 1 :]], axis=0)
    pair_w = jnp.concatenate([pair_w[0::2], pair_w[1::2]], axis=2)

    sent = conv_send(idx, z_place, ext_rows, pair_w, conv_weight[PAIRS], norm_gains[0:1])
    returned = block(
        True, slots[0], exchange(sent), qkv_weight[0], out_weight[0], up_weight[0],
        down_weight[0], norm_gains[1], norm_gains[2],
    )
    resent = relay(z_place, h_place, exchange(returned))
    return block(
        False, slots[1], exchange(resent), qkv_weight[1], out_weight[1], up_weight[1],
        down_weight[1], norm_gains[3], norm_gains[4],
    )


def solution(mesh):
    placed = (
        P(None, ("gx", "gy")),
        P(("gx", "gy"), None, None),
        P(None, ("gx", "gy")),
        P(None, ("gx", "gy")),
        P(None, ("gx", "gy")),
        P(),
        P(),
        P(),
        P(),
        P(),
        P(),
    )
    return jax.shard_map(
        local, mesh=mesh, in_specs=placed, out_specs=P(None, ("gx", "gy")), check_vma=False
    )
```

time: 941 us -> 325 us (0.35); the launches traced: 931 us -> 325 us
  local copies, waits for them, and re-layouts: 531 us -> 18 us
  matrix products: 260 us -> 2.59 us
  Pallas kernels: 0 us -> 216 us
  other arithmetic: 40.3 us -> 5.31 us
  starting transfers between devices: 51.8 us -> 42.2 us
    gather x3 -> x0, local copies, waits for them, and re-layouts: 431 us -> none  [the longest x2 409 us: positional(): jnp.take(ext_rows, resolved.reshape(-1), axis=0)]
    dot_general x43 -> x4, matrix products: 219 us -> 2.59 us  [the longest x2 1.6 us: places(): jnp.einsum('dbi,ij->dbj', grouped, strict, preferred_element_type=F32)]
    pallas_call x0 -> x4, Pallas kernels: none -> 216 us  [the longest x1 121 us: conv_send(): pl.pallas_call(conv_kernel, grid=(steps,), in_specs=[pl.BlockSpec((2 * PA...]
    scatter x5 -> x0, local copies, waits for them, and re-layouts: 75.1 us -> none  [the longest x2 32.5 us: send_out(): jnp.zeros((points + 1, channels), rows.dtype).at[slot_in].set(arrived.T)]
    sub x8 -> x0, matrix products: 41.5 us -> none  [patch_block(): weights = jnp.exp(scores - row_max)]
    scatter x1 -> x0, other arithmetic: 26.9 us -> none  [send_out(): jnp.zeros((devices * capacity, channels), rows.dtype).at[packed].set(rows)]
    all_to_all x5 -> x4, starting transfers between devices: 40.9 us -> 32.2 us  [the longest x3 20.7 us: exchange(): lax.all_to_all(shaped, ('gx', 'gy'), split_axis=0, concat_axis=0, tiled=T...]
    all_to_all x5 -> x4, waiting for transfers between devices: 45.5 us -> 40.1 us  [the longest x3 40.1 us: exchange(): lax.all_to_all(shaped, ('gx', 'gy'), split_axis=0, concat_axis=0, tiled=T...]
  transfers between devices with their start and end apart: 9 -> 8, of which waited for: 3 -> 3; matrix products, arithmetic and copies ran while one was open for 69% -> 5% of each run, Pallas kernels for 0% -> 37%
where the time goes in v1:
time: 325 us
  Pallas kernels  216 us (66%)
  starting transfers between devices  42.2 us (13%)
  waiting for transfers between devices  40.1 us (12%)
  local copies, waits for them, and re-layouts  18 us (6%)
  other arithmetic  5.31 us (2%)
    pallas_call x1, Pallas kernels, conv_send(): pl.pallas_call(conv_kernel, grid=(steps,), in_specs=[pl.BlockSpec((2 * PA...  121 us
    pallas_call x2, Pallas kernels, block(): pl.pallas_call(functools.partial(block_kernel, back), in_specs=[pl.BlockS...  83.9 us
    all_to_all x3, waiting for transfers between devices, exchange(): lax.all_to_all(shaped, ('gx', 'gy'), split_axis=0, concat_axis=0, tiled=T...  40.1 us
    all_to_all x3, starting transfers between devices, exchange(): lax.all_to_all(shaped, ('gx', 'gy'), split_axis=0, concat_axis=0, tiled=T...  20.7 us
    all_to_all x1, starting transfers between devices, local(): lax.all_to_all(jnp.concatenate([z_list, h_list], axis=1), ('gx', 'gy'), s...  11.5 us
    pallas_call x1, Pallas kernels, relay(): pl.pallas_call(relay_kernel, in_specs=[pl.BlockSpec(memory_space=pltpu.SM...  10.9 us
    unnamed x43, local copies, waits for them, and re-layouts  9.49 us
    ppermute x2, starting transfers between devices, beside(): low = lax.ppermute(block_cols[:, 1], axis, forward)  6.76 us
  transfers between devices with their start and end apart: 8, of which 3 were waited for; matrix products, arithmetic and copies ran while one was open for 5% of the time, Pallas kernels for 37%

profile of v1, /device:TPU:1, one launch (start us, length us, event | category | flops | bytes accessed | tf_op | source)
XLA Modules:
  0.0 324.7 jit_solution(12190198720613317551)
XLA Ops:
  0.0 0.9 slice_add_fusion.3
  1.3 0.8 fusion
  6.2 11.5 %all-to-all-start = ((s32[128,1,96]{2,1,0:T(1,128)}), s32[128,1,96]{2,1,0:T(1,128)S(1)}, u32[]{:S(2)}, u32[]{:S(2)}) async-start(s32[128,1,96]{2,1,0:T(1,128)} %copy.67), calls=%async_computation | async-start | bytes 131072 | tf_op jit(solution)/shard_map/all_to_all | solution.py:325
  18.2 1.3 gather_fusion
  19.7 3.7 %collective-permute-start = (bf16[64,128]{0,1:T(8,128)(2,1)S(1)}, bf16[64,128]{0,1:T(8,128)(2,1)S(1)}, u32[]{:S(2)}, u32[]{:S(2)}) collective-permute-start(bf16[64,128]{0,1:T(8,128)(2,1)S(1)} %get-tuple-element.14), channel_id=1, source_target_pairs={{0,16},{16,32},{32,48},{48,64},{64,80},{80,96},{96,112},{1,17},{17... | collective-permute-start | bytes 49160 | tf_op jit(solution)/shard_map/ppermute | solution.py:270
  23.4 1.9 collective-permute-start.1
  25.4 3.1 collective-permute-start.2
  28.5 1.3 collective-permute-start.3
  32.0 0.9 fusion.24.idx_ref
  32.9 0.8 pad_maximum_fusion.1.pair_ref
  33.8 1.0 copy-done
  34.9 121.3 %conv_send.1 = bf16[3072,128]{1,0:T(8,128)(2,1)} custom-call(s32[26,4096]{1,0:T(8,128)} %fusion.24.idx_ref, s32[4096]{0:T(1024)} %fusion.34.place_ref.from_ref, bf16[4608,64]{1,0:T(8,128)(2,1)} %bitcast.85, bf16[13,64,128]{2,1,0:T(8,128)(2,1)} %pad_maximum_fusion.1.pair_ref, bf16[64,64]{1,0:T(8,128)(2,1)} %slice_bitcast_fusion.6.self_ref, ...), custom_call_target="tpu_custom_call" | custom-call | flops 99999997952 | bytes 1000000 | tf_op jit(solution)/shard_map/conv_send/pallas_call | solution.py:125
  156.2 12.3 %all-to-all-start.1 = ((bf16[128,24,128]{2,1,0:T(8,128)(2,1)}), bf16[128,24,128]{2,1,0:T(8,128)(2,1)S(1)}, u32[]{:S(2)}, u32[]{:S(2)}) async-start(bf16[128,24,128]{2,1,0:T(8,128)(2,1)} %bitcast.86), calls=%async_computation.1 | async-start | bytes 1572864 | tf_op jit(solution)/shard_map/all_to_all | solution.py:301
  173.6 11.5 %all-to-all-done.1 = bf16[128,24,128]{2,1,0:T(8,128)(2,1)S(1)} async-done(((bf16[128,24,128]{2,1,0:T(8,128)(2,1)}), bf16[128,24,128]{2,1,0:T(8,128)(2,1)S(1)}, u32[]{:S(2)}, u32[]{:S(2)}) %all-to-all-start.1) | async-done | bytes 786464 | tf_op jit(solution)/shard_map/all_to_all | solution.py:301
  185.1 0.9 copy-done.1
  186.1 45.6 %block_back.1 = bf16[3072,128]{1,0:T(8,128)(2,1)} custom-call(s32[6144]{0:T(1024)} %squeeze.55.slot_ref, bf16[3072,128]{1,0:T(8,128)(2,1)} %bitcast.87, bf16[192,64]{1,0:T(8,128)(2,1)} %bitcast.106, bf16[64,64]{1,0:T(8,128)(2,1)} %bitcast.108, bf16[256,64]{1,0:T(8,128)(2,1)} %bitcast.102, bf16[64,256]{1,0:T(8,128)(2,1)} %get-tuple-element.16.down_ref, ...), custom_call_target="tpu_custom_call" | custom-call | flops 40000000000 | bytes 1000000 | tf_op jit(solution)/shard_map/block_back/pallas_call | solution.py:248
  231.7 4.3 %all-to-all-start.2 = ((bf16[128,24,128]{2,1,0:T(8,128)(2,1)}), bf16[128,24,128]{2,1,0:T(8,128)(2,1)S(1)}, u32[]{:S(2)}, u32[]{:S(2)}) async-start(bf16[128,24,128]{2,1,0:T(8,128)(2,1)} %bitcast.90), calls=%async_computation.2 | async-start | bytes 1572864 | tf_op jit(solution)/shard_map/all_to_all | solution.py:301
  236.6 16.2 %all-to-all-done.2 = bf16[128,24,128]{2,1,0:T(8,128)(2,1)S(1)} async-done(((bf16[128,24,128]{2,1,0:T(8,128)(2,1)}), bf16[128,24,128]{2,1,0:T(8,128)(2,1)S(1)}, u32[]{:S(2)}, u32[]{:S(2)}) %all-to-all-start.2) | async-done | bytes 786464 | tf_op jit(solution)/shard_map/all_to_all | solution.py:301
  252.8 0.9 copy-done.3
  253.7 10.9 %relay.1 = bf16[3072,128]{1,0:T(8,128)(2,1)} custom-call(s32[4096]{0:T(1024)} %fusion.34.place_ref.from_ref, s32[4096]{0:T(1024)} %fusion.37.to_ref, bf16[3072,128]{1,0:T(8,128)(2,1)} %bitcast.91), custom_call_target="tpu_custom_call" | custom-call | flops 1000000000 | bytes 1000000 | tf_op jit(solution)/shard_map/relay/pallas_call | solution.py:163
  264.6 4.2 %all-to-all-start.3 = ((bf16[128,24,128]{2,1,0:T(8,128)(2,1)}), bf16[128,24,128]{2,1,0:T(8,128)(2,1)S(1)}, u32[]{:S(2)}, u32[]{:S(2)}) async-start(bf16[128,24,128]{2,1,0:T(8,128)(2,1)} %bitcast.89), calls=%async_computation.3 | async-start | bytes 1572864 | tf_op jit(solution)/shard_map/all_to_all | solution.py:301
  273.1 12.4 %all-to-all-done.3 = bf16[128,24,128]{2,1,0:T(8,128)(2,1)S(1)} async-done(((bf16[128,24,128]{2,1,0:T(8,128)(2,1)}), bf16[128,24,128]{2,1,0:T(8,128)(2,1)S(1)}, u32[]{:S(2)}, u32[]{:S(2)}) %all-to-all-start.3) | async-done | bytes 786464 | tf_op jit(solution)/shard_map/all_to_all | solution.py:301
  285.6 0.9 copy-done.2
  286.4 38.3 %block_last.1 = bf16[64,4096]{1,0:T(8,128)(2,1)} custom-call(s32[6144]{0:T(1024)} %squeeze.54.slot_ref, bf16[3072,128]{1,0:T(8,128)(2,1)} %bitcast.88, bf16[192,64]{1,0:T(8,128)(2,1)} %bitcast.107, bf16[64,64]{1,0:T(8,128)(2,1)} %bitcast.109, bf16[256,64]{1,0:T(8,128)(2,1)} %bitcast.103, bf16[64,256]{1,0:T(8,128)(2,1)} %get-tuple-element.15.down_ref, ...), custom_call_target="tpu_custom_call" | custom-call | flops 40000000000 | bytes 1000000 | tf_op jit(solution)/shard_map/block_last/pallas_call | solution.py:248
  (93 shorter events, 17.4 us)
Async XLA Ops:
  2.3 0.8 copy-start.12
  4.3 0.6 copy-start.7
  4.9 12.8 %copy-start.14 = (s32[1,4,128]{2,1,0:T(4,128)S(1)}, s32[1,4,128]{2,1,0:T(4,128)}, u32[]{:S(2)}) copy-start(s32[1,4,128]{2,1,0:T(4,128)} %param.12) | copy-start | bytes 6148
  4.9 12.8 %copy-start.4 = (bf16[64,4096]{1,0:T(8,128)(2,1)S(1)}, bf16[64,4096]{1,0:T(8,128)(2,1)}, u32[]{:S(2)}) copy-start(bf16[64,4096]{1,0:T(8,128)(2,1)} %param.11) | copy-start | bytes 1572868
  6.2 150.0 %all-to-all-start = ((s32[128,1,96]{2,1,0:T(1,128)}), s32[128,1,96]{2,1,0:T(1,128)S(1)}, u32[]{:S(2)}, u32[]{:S(2)}) async-start(s32[128,1,96]{2,1,0:T(1,128)} %copy.67), calls=%async_computation | async-start | bytes 131072 | tf_op jit(solution)/shard_map/all_to_all | solution.py:325
  19.7 10.7 %copy-start.6 = (bf16[27,64,64]{2,1,0:T(8,128)(2,1)S(1)}, bf16[27,64,64]{2,1,0:T(8,128)(2,1)}, u32[]{:S(2)}) copy-start(bf16[27,64,64]{2,1,0:T(8,128)(2,1)} %param.16) | copy-start | bytes 663556
  19.7 14.0 %collective-permute-start = (bf16[64,128]{0,1:T(8,128)(2,1)S(1)}, bf16[64,128]{0,1:T(8,128)(2,1)S(1)}, u32[]{:S(2)}, u32[]{:S(2)}) collective-permute-start(bf16[64,128]{0,1:T(8,128)(2,1)S(1)} %get-tuple-element.14), channel_id=1, source_target_pairs={{0,16},{16,32},{32,48},{48,64},{64,80},{80,96},{96,112},{1,17},{17... | collective-permute-start | bytes 49160 | tf_op jit(solution)/shard_map/ppermute | solution.py:270
  23.4 10.3 %collective-permute-start.1 = (bf16[64,128]{0,1:T(8,128)(2,1)S(1)}, bf16[64,128]{0,1:T(8,128)(2,1)S(1)}, u32[]{:S(2)}, u32[]{:S(2)}) collective-permute-start(bf16[64,128]{0,1:T(8,128)(2,1)S(1)} %get-tuple-element.13), channel_id=1, source_target_pairs={{16,0},{32,16},{48,32},{64,48},{80,64},{96,80},{112,96},{17,1},{33... | collective-permute-start | bytes 49160 | tf_op jit(solution)/shard_map/ppermute | solution.py:271
  25.4 8.4 %collective-permute-start.2 = (bf16[64,128]{0,1:T(8,128)(2,1)S(1)}, bf16[64,128]{0,1:T(8,128)(2,1)S(1)}, u32[]{:S(2)}, u32[]{:S(2)}) collective-permute-start(bf16[64,128]{0,1:T(8,128)(2,1)S(1)} %get-tuple-element.12), channel_id=1, source_target_pairs={{0,1},{1,2},{2,3},{3,4},{4,5},{5,6},{6,7},{7,8},{8,9},{9,10},{10,1... | collective-permute-start | bytes 49160 | tf_op jit(solution)/shard_map/ppermute | solution.py:270
  28.5 5.3 %collective-permute-start.3 = (bf16[64,128]{0,1:T(8,128)(2,1)S(1)}, bf16[64,128]{0,1:T(8,128)(2,1)S(1)}, u32[]{:S(2)}, u32[]{:S(2)}) collective-permute-start(bf16[64,128]{0,1:T(8,128)(2,1)S(1)} %get-tuple-element.11), channel_id=1, source_target_pairs={{1,0},{2,1},{3,2},{4,3},{5,4},{6,5},{7,6},{8,7},{9,8},{10,9},{11,1... | collective-permute-start | bytes 49160 | tf_op jit(solution)/shard_map/ppermute | solution.py:271
  30.5 0.8 copy-start.15
  30.5 1.4 copy-start.5
  31.1 0.9 copy-start.9
  33.8 1.1 copy-start
  156.2 12.3 %copy-start.10 = (bf16[2,64,192]{2,1,0:T(8,128)(2,1)S(1)}, bf16[2,64,192]{2,1,0:T(8,128)(2,1)}, u32[]{:S(2)}) copy-start(bf16[2,64,192]{2,1,0:T(8,128)(2,1)} %param.17) | copy-start | bytes 147460
  156.2 15.2 %copy-start.13 = (bf16[2,64,64]{2,1,0:T(8,128)(2,1)S(1)}, bf16[2,64,64]{2,1,0:T(8,128)(2,1)}, u32[]{:S(2)}) copy-start(bf16[2,64,64]{2,1,0:T(8,128)(2,1)} %param.18) | copy-start | bytes 49156
  156.2 15.9 %copy-start.11 = (bf16[2,256,64]{1,2,0:T(8,128)(2,1)S(1)}, bf16[2,256,64]{1,2,0:T(8,128)(2,1)}, u32[]{:S(2)}) copy-start(bf16[2,256,64]{1,2,0:T(8,128)(2,1)} %param.20) | copy-start | bytes 196612
  156.2 28.9 %all-to-all-start.1 = ((bf16[128,24,128]{2,1,0:T(8,128)(2,1)}), bf16[128,24,128]{2,1,0:T(8,128)(2,1)S(1)}, u32[]{:S(2)}, u32[]{:S(2)}) async-start(bf16[128,24,128]{2,1,0:T(8,128)(2,1)} %bitcast.86), calls=%async_computation.1 | async-start | bytes 1572864 | tf_op jit(solution)/shard_map/all_to_all | solution.py:301
  185.1 0.9 copy-start.1
  231.7 4.3 %copy-start.8 = (f32[32,128]{1,0:T(8,128)S(1)}, f32[32,128]{1,0:T(8,128)}, u32[]{:S(2)}) copy-start(f32[32,128]{1,0:T(8,128)} %copy-done.7) | copy-start | bytes 49156
  231.7 21.1 %all-to-all-start.2 = ((bf16[128,24,128]{2,1,0:T(8,128)(2,1)}), bf16[128,24,128]{2,1,0:T(8,128)(2,1)S(1)}, u32[]{:S(2)}, u32[]{:S(2)}) async-start(bf16[128,24,128]{2,1,0:T(8,128)(2,1)} %bitcast.90), calls=%async_computation.2 | async-start | bytes 1572864 | tf_op jit(solution)/shard_map/all_to_all | solution.py:301
  252.8 0.9 copy-start.3
  264.6 21.0 %all-to-all-start.3 = ((bf16[128,24,128]{2,1,0:T(8,128)(2,1)}), bf16[128,24,128]{2,1,0:T(8,128)(2,1)S(1)}, u32[]{:S(2)}, u32[]{:S(2)}) async-start(bf16[128,24,128]{2,1,0:T(8,128)(2,1)} %bitcast.89), calls=%async_computation.3 | async-start | bytes 1572864 | tf_op jit(solution)/shard_map/all_to_all | solution.py:301
  285.6 0.9 copy-start.2

commit v2 on v1

--- a/solution.py
+++ b/solution.py
@@ -21,7 +21,12 @@
 PACK = DEV * HALF
 PAIRS = 13
 BLK = 512
-UN = 8
+UN = 16
+GROUP = 32
+GROUPS = PTS // GROUP
+LISTS = 4
+LOG2_E = 1.4426950408889634
+SAFE = 72.0
 EPS = 1e-05
 VMEM = 60 * 2**20
 BF = jnp.bfloat16
@@ -68,78 +73,90 @@
     lax.fori_loop(0, PACK // 512, part, 0)
 
 
-def conv_kernel(idx_ref, place_ref, ext_ref, pair_ref, self_ref, gain_ref, out_ref, table, sums, rows):
-    step = pl.program_id(0)
-
-    @pl.when(step == 0)
-    def _():
-        def fill(b, _):
-            at = pl.multiple_of(b * 512, 512)
-            chunk = ext_ref[pl.ds(at, 512), :]
-            for j in range(PAIRS):
-                table[pl.ds(pl.multiple_of(j * TROWS + at, 8), 512), :] = jnp.dot(
-                    chunk, pair_ref[j], preferred_element_type=F32
-                )
-            return 0
-
-        lax.fori_loop(0, EXT // 512, fill, 0)
+def move_rows(count, read, place_ref, rows_ref):
+    def move(g, _):
+        at = g * UN
+        taken = [read(at + u) for u in range(UN)]
+        for u in range(UN):
+            rows_ref[pl.ds(place_ref[at + u], 1), :] = taken[u]
+        return 0
+
+    lax.fori_loop(0, count // UN, move, 0)
+
+
+def conv_kernel(idx_ref, place_ref, ext_ref, pair_ref, self_ref, gain_ref, out_ref, *scratch):
+    table, sums, rows = scratch[:3]
+    lists, sems = scratch[3 : 3 + LISTS], scratch[3 + LISTS]
+
+    def list_copy(g, b):
+        return pltpu.make_async_copy(idx_ref.at[g], lists[b], sems.at[b])
+
+    for b in range(LISTS):
+        list_copy(b, b).start()
+
+    def fill(b, _):
+        at = pl.multiple_of(b * 512, 512)
+        chunk = ext_ref[pl.ds(at, 512), :]
         for j in range(PAIRS):
-            table[j * TROWS + EXT : (j + 1) * TROWS, :] = jnp.zeros((TROWS - EXT, 128), F32)
+            table[pl.ds(pl.multiple_of(j * TROWS + at, 8), 512), :] = jnp.dot(
+                chunk, pair_ref[j], preferred_element_type=F32
+            )
+        return 0
+
+    lax.fori_loop(0, EXT // 512, fill, 0)
+    for j in range(PAIRS):
+        table[j * TROWS + EXT : (j + 1) * TROWS, :] = jnp.zeros((TROWS - EXT, 128), F32)
 
     low_row = low_lanes(1)
 
-    def gather(g, _):
-        for u in range(UN):
-            i = g * UN + u
-            even, odd = None, None
-            for j in range(PAIRS):
-                a = table[pl.ds(idx_ref[2 * j, i], 1), :]
-                b = table[pl.ds(idx_ref[2 * j + 1, i], 1), :]
-                even = a if even is None else even + a
-                odd = b if odd is None else odd + b
-            sums[pl.ds(i, 1), :] = jnp.where(low_row, even, odd)
-        return 0
-
-    lax.fori_loop(0, BLK // UN, gather, 0)
-    own = ext_ref[pl.ds(pl.multiple_of(step * BLK, BLK), BLK), :]
-    both = sums[...]
-    conv = both[:, :C] + both[:, C:] + jnp.dot(own, self_ref[...], preferred_element_type=F32)
-    encoded = own.astype(F32) + lane_norm(conv, gain_ref[...])
-    sums[:, :C] = encoded
-
-    def scatter(g, _):
-        for u in range(UN):
-            i = g * UN + u
-            rows[pl.ds(place_ref[step * BLK + i], 1), :] = sums[pl.ds(i, 1), :]
-        return 0
-
-    lax.fori_loop(0, BLK // UN, scatter, 0)
-
-    @pl.when(step == pl.num_programs(0) - 1)
-    def _():
-        pack_rows(rows, out_ref)
+    def gather(step, _):
+        for b in range(LISTS):
+            g = step * LISTS + b
+            list_copy(g, b).wait()
+            for u in range(GROUP):
+                even, odd = None, None
+                for j in range(PAIRS):
+                    at = 2 * j * GROUP + u
+                    first = table[pl.ds(lists[b][at // 128, at % 128], 1), :]
+                    at = at + GROUP
+                    second = table[pl.ds(lists[b][at // 128, at % 128], 1), :]
+                    even = first if even is None else even + first
+                    odd = second if odd is None else odd + second
+                sums[pl.ds(u * GROUPS + g, 1), :] = jnp.where(low_row, even, odd)
+            list_copy(jnp.minimum(g + LISTS, GROUPS - 1), b).start()
+        return 0
+
+    lax.fori_loop(0, GROUPS // LISTS, gather, 0)
+    for b in range(LISTS):
+        list_copy(GROUPS - 1, b).wait()
+
+    def finish(b, _):
+        at = pl.multiple_of(b * BLK, BLK)
+        own = ext_ref[pl.ds(at, BLK), :]
+        both = sums[pl.ds(at, BLK), :]
+        conv = both[:, :C] + both[:, C:] + jnp.dot(own, self_ref[...], preferred_element_type=F32)
+        sums[pl.ds(at, BLK), :C] = own.astype(F32) + lane_norm(conv, gain_ref[...])
+        return 0
+
+    lax.fori_loop(0, PTS // BLK, finish, 0)
+    move_rows(PTS, lambda i: sums[pl.ds(i, 1), :], place_ref, rows)
+    pack_rows(rows, out_ref)
 
 
 def conv_send(idx, place, ext_rows, pair_w, self_w, gain):
-    steps = PTS // BLK
     return pl.pallas_call(
         conv_kernel,
-        grid=(steps,),
-        in_specs=[
-            pl.BlockSpec((2 * PAIRS, BLK), lambda s: (0, s), memory_space=pltpu.SMEM),
-            pl.BlockSpec(memory_space=pltpu.SMEM),
-            pl.BlockSpec((EXT, C), lambda s: (0, 0)),
-            pl.BlockSpec((PAIRS, C, 128), lambda s: (0, 0, 0)),
-            pl.BlockSpec((C, C), lambda s: (0, 0)),
-            pl.BlockSpec((1, C), lambda s: (0, 0)),
-        ],
-        out_specs=pl.BlockSpec((PACK, 128), lambda s: (0, 0)),
+        in_specs=[pl.BlockSpec(memory_space=pl.ANY), pl.BlockSpec(memory_space=pltpu.SMEM)]
+        + [pl.BlockSpec(memory_space=pltpu.VMEM)] * 4,
+        out_specs=pl.BlockSpec(memory_space=pltpu.VMEM),
         out_shape=jax.ShapeDtypeStruct((PACK, 128), BF),
         scratch_shapes=[
             pltpu.VMEM((PAIRS * TROWS, 128), F32),
-            pltpu.VMEM((BLK, 128), F32),
+            pltpu.VMEM((PTS, 128), F32),
             pltpu.VMEM((2 * PACK, 128), F32),
-        ],
+        ]
+        + [pltpu.SMEM((8, 128), jnp.int32)] * LISTS
+        + [pltpu.SemaphoreType.DMA((LISTS,))],
         compiler_params=pltpu.CompilerParams(vmem_limit_bytes=VMEM),
         cost_estimate=pl.CostEstimate(flops=10**11, bytes_accessed=10**6, transcendentals=0),
         name="conv_send",
@@ -149,13 +166,7 @@
 def relay_kernel(from_ref, to_ref, in_ref, out_ref, source, target):
     unpack_rows(in_ref, source)
 
-    def move(g, _):
-        for u in range(UN):
-            i = g * UN + u
-            target[pl.ds(to_ref[i], 1), :] = source[pl.ds(from_ref[i], 1), :]
-        return 0
-
-    lax.fori_loop(0, PTS // UN, move, 0)
+    move_rows(PTS, lambda i: source[pl.ds(from_ref[i], 1), :], to_ref, target)
     pack_rows(target, out_ref)
 
 
@@ -182,20 +193,49 @@
 def patch_math(x, qkv_ref, outw_ref, up_ref, down_ref, gain_a_ref, gain_b_ref, mixed):
     normed = chan_norm(x, gain_a_ref[...]).astype(BF)
     qkv = jnp.dot(qkv_ref[...], normed, preferred_element_type=F32).astype(BF)
-    queries = qkv[:C].astype(F32) * HEAD_DIM**-0.5
-    keys = qkv[C : 2 * C].astype(F32).T.astype(BF)
+    queries = qkv[:C].astype(F32)
+    keys = qkv[C : 2 * C].astype(F32)
+    keys_t = keys.T
     head_of = lax.broadcasted_iota(jnp.int32, (C, PATCH), 0) // HEAD_DIM
     ones = jnp.ones((HEAD_DIM, PATCH), BF)
-    for h in range(HEADS):
-        masked = jnp.where(head_of == h, queries, 0.0).astype(BF)
-        scores = jnp.dot(keys, masked, preferred_element_type=F32)
-        weights = jnp.exp(scores - jnp.max(scores, axis=0, keepdims=True)).astype(BF)
+
+    def of_head(h, values):
+        return jnp.where(head_of == h, values, 0.0)
+
+    def mix(h, weights):
         first = 2 * C + h * HEAD_DIM
         values = jnp.concatenate([qkv[first : first + HEAD_DIM], ones], axis=0)
         summed = jnp.dot(values, weights, preferred_element_type=F32)
         mixed[h * HEAD_DIM : (h + 1) * HEAD_DIM, :] = (
             summed[:HEAD_DIM] / summed[HEAD_DIM : HEAD_DIM + 1]
         ).astype(BF)
+
+    def longest(values):
+        squares = (values * values).reshape(HEADS, HEAD_DIM, PATCH)
+        return jnp.max(jnp.sum(squares, axis=1), axis=1, keepdims=True)
+
+    reach = jnp.max(longest(queries) * longest(keys))
+    safe = reach <= (SAFE * HEAD_DIM**0.5) ** 2
+
+    @pl.when(safe)
+    def _():
+        scaled = queries * (HEAD_DIM**-0.5 * LOG2_E)
+        upper = scaled.astype(BF).astype(F32)
+        lower = scaled - upper
+        keys_2 = jnp.concatenate([keys_t, keys_t], axis=1).astype(BF)
+        for h in range(HEADS):
+            split = jnp.concatenate([of_head(h, upper), of_head(h, lower)], axis=0).astype(BF)
+            scores = jnp.dot(keys_2, split, preferred_element_type=F32)
+            mix(h, jnp.exp2(scores).astype(BF))
+
+    @pl.when(jnp.logical_not(safe))
+    def _():
+        keys_1 = keys_t.astype(BF)
+        for h in range(HEADS):
+            one_head = of_head(h, queries * HEAD_DIM**-0.5).astype(BF)
+            scores = jnp.dot(keys_1, one_head, preferred_element_type=F32)
+            mix(h, jnp.exp(scores - jnp.max(scores, axis=0, keepdims=True)).astype(BF))
+
     residual = x + jnp.dot(outw_ref[...], mixed[...], preferred_element_type=F32)
     normed_b = chan_norm(residual, gain_b_ref[...]).astype(BF)
     raised = jnp.dot(up_ref[...], normed_b, preferred_element_type=F32)
@@ -209,13 +249,7 @@
 ):
     unpack_rows(in_ref, source)
 
-    def place(g, _):
-        for u in range(UN):
-            i = g * UN + u
-            rows[pl.ds(slot_ref[i], 1), :] = source[pl.ds(i, 1), :]
-        return 0
-
-    lax.fori_loop(0, 2 * PACK // UN, place, 0)
+    move_rows(2 * PACK, lambda i: source[pl.ds(i, 1), :], slot_ref, rows)
 
     def patch(p, _):
         at = pl.multiple_of(p * PATCH, PATCH)
@@ -232,11 +266,14 @@
         low_row = low_lanes(1)
 
         def fetch(g, _):
+            at = g * UN
+            taken = []
             for u in range(UN):
-                i = g * UN + u
-                low = rows[pl.ds(slot_ref[i], 1), :]
-                high = rows[pl.ds(slot_ref[i + PACK], 1), :]
-                source[pl.ds(i, 1), :] = jnp.where(low_row, low, high)
+                low = rows[pl.ds(slot_ref[at + u], 1), :]
+                high = rows[pl.ds(slot_ref[at + u + PACK], 1), :]
+                taken.append(jnp.where(low_row, low, high))
+            for u in range(UN):
+                source[pl.ds(at + u, 1), :] = taken[u]
             return 0
 
         lax.fori_loop(0, PACK // UN, fetch, 0)
@@ -331,6 +368,8 @@
     others = jnp.concatenate([neighbours[:PAIRS], neighbours[PAIRS + 1 :]], axis=0)
     base = (jnp.arange(2 * PAIRS, dtype=jnp.int32) // 2 * TROWS)[:, None]
     idx = jnp.where(others < 0, EXT, others) + base
+    idx = jnp.pad(idx, ((0, 1024 // GROUP - 2 * PAIRS), (0, 0)))
+    idx = idx.reshape(1024, GROUPS).T.reshape(GROUPS, 8, 128)
     pair_w = jnp.concatenate([conv_weight[:PAIRS], conv_weight[PAIRS + 1 :]], axis=0)
     pair_w = jnp.concatenate([pair_w[0::2], pair_w[1::2]], axis=2)
 

time: 325 us -> 276 us (0.85)
  Pallas kernels: 216 us -> 167 us
    pallas_call x1, Pallas kernels: 121 us -> 75.1 us  [conv_send(): pl.pallas_call(conv_kernel, in_specs=[pl.BlockSpec(memory_space=pl.ANY),...]
    unnamed x43 -> x48, local copies, waits for them, and re-layouts: 9.49 us -> 9.91 us
  transfers between devices with their start and end apart: 8 -> 8, of which waited for: 3 -> 3; matrix products, arithmetic and copies ran while one was open for 5% -> 6% of each run, Pallas kernels for 37% -> 27%
where the time goes in v2:
time: 276 us
  Pallas kernels  167 us (61%)
  starting transfers between devices  41.8 us (15%)
  waiting for transfers between devices  40.2 us (15%)
  local copies, waits for them, and re-layouts  18.7 us (7%)
  other arithmetic  4.52 us (2%)
    pallas_call x2, Pallas kernels, block(): pl.pallas_call(functools.partial(block_kernel, back), in_specs=[pl.BlockS...  82.5 us
    pallas_call x1, Pallas kernels, conv_send(): pl.pallas_call(conv_kernel, in_specs=[pl.BlockSpec(memory_space=pl.ANY),...  75.1 us
    all_to_all x3, waiting for transfers between devices, exchange(): lax.all_to_all(shaped, ('gx', 'gy'), split_axis=0, concat_axis=0, tiled=T...  40.1 us
    all_to_all x3, starting transfers between devices, exchange(): lax.all_to_all(shaped, ('gx', 'gy'), split_axis=0, concat_axis=0, tiled=T...  20.3 us
    all_to_all x1, starting transfers between devices, local(): lax.all_to_all(jnp.concatenate([z_list, h_list], axis=1), ('gx', 'gy'), s...  11.5 us
    unnamed x48, local copies, waits for them, and re-layouts  9.91 us
    pallas_call x1, Pallas kernels, relay(): pl.pallas_call(relay_kernel, in_specs=[pl.BlockSpec(memory_space=pltpu.SM...  9.8 us
    ppermute x2, starting transfers between devices, beside(): low = lax.ppermute(block_cols[:, 1], axis, forward)  6.76 us
  transfers between devices with their start and end apart: 8, of which 3 were waited for; matrix products, arithmetic and copies ran while one was open for 6% of the time, Pallas kernels for 27%

profile of v2, /device:TPU:1, one launch (start us, length us, event | category | flops | bytes accessed | tf_op | source)
XLA Modules:
  0.0 275.6 jit_solution(14760141582264223322)
XLA Ops:
  0.0 0.9 slice_add_fusion.3
  1.3 0.8 fusion
  5.8 11.5 %all-to-all-start = ((s32[128,1,96]{2,1,0:T(1,128)}), s32[128,1,96]{2,1,0:T(1,128)S(1)}, u32[]{:S(2)}, u32[]{:S(2)}) async-start(s32[128,1,96]{2,1,0:T(1,128)} %copy.71), calls=%async_computation | async-start | bytes 131072 | tf_op jit(solution)/shard_map/all_to_all | solution.py:362
  17.9 1.3 gather_fusion
  19.4 3.7 %collective-permute-start = (bf16[64,128]{0,1:T(8,128)(2,1)S(1)}, bf16[64,128]{0,1:T(8,128)(2,1)S(1)}, u32[]{:S(2)}, u32[]{:S(2)}) collective-permute-start(bf16[64,128]{0,1:T(8,128)(2,1)S(1)} %get-tuple-element.14), channel_id=1, source_target_pairs={{0,16},{16,32},{32,48},{48,64},{64,80},{80,96},{96,112},{1,17},{17... | collective-permute-start | bytes 49160 | tf_op jit(solution)/shard_map/ppermute | solution.py:307
  23.1 1.9 collective-permute-start.1
  25.0 3.1 %collective-permute-start.2 = (bf16[64,128]{0,1:T(8,128)(2,1)S(1)}, bf16[64,128]{0,1:T(8,128)(2,1)S(1)}, u32[]{:S(2)}, u32[]{:S(2)}) collective-permute-start(bf16[64,128]{0,1:T(8,128)(2,1)S(1)} %get-tuple-element.12), channel_id=1, source_target_pairs={{0,1},{1,2},{2,3},{3,4},{4,5},{5,6},{6,7},{7,8},{8,9},{9,10},{10,1... | collective-permute-start | bytes 49160 | tf_op jit(solution)/shard_map/ppermute | solution.py:307
  28.1 1.3 collective-permute-start.3
  31.7 0.8 pad_maximum_fusion.1.pair_ref
  32.9 0.9 copy.94
  33.9 1.0 copy-done
  34.9 75.1 %conv_send.1 = bf16[3072,128]{1,0:T(8,128)(2,1)} custom-call(s32[128,8,128]{2,1,0:T(8,128)} %bitcast.96, s32[4096]{0:T(1024)} %fusion.34.place_ref.from_ref, bf16[4608,64]{1,0:T(8,128)(2,1)} %bitcast.89, bf16[13,64,128]{2,1,0:T(8,128)(2,1)} %pad_maximum_fusion.1.pair_ref, bf16[64,64]{1,0:T(8,128)(2,1)} %slice_bitcast_fusion.6.self_ref, ...), custom_call_target="tpu_custom_call" | custom-call | flops 99999997952 | bytes 1000000 | tf_op jit(solution)/shard_map/conv_send/pallas_call | solution.py:147
  110.0 11.8 %all-to-all-start.1 = ((bf16[128,24,128]{2,1,0:T(8,128)(2,1)}), bf16[128,24,128]{2,1,0:T(8,128)(2,1)S(1)}, u32[]{:S(2)}, u32[]{:S(2)}) async-start(bf16[128,24,128]{2,1,0:T(8,128)(2,1)} %bitcast.90), calls=%async_computation.1 | async-start | bytes 1572864 | tf_op jit(solution)/shard_map/all_to_all | solution.py:338
  127.0 11.5 %all-to-all-done.1 = bf16[128,24,128]{2,1,0:T(8,128)(2,1)S(1)} async-done(((bf16[128,24,128]{2,1,0:T(8,128)(2,1)}), bf16[128,24,128]{2,1,0:T(8,128)(2,1)S(1)}, u32[]{:S(2)}, u32[]{:S(2)}) %all-to-all-start.1) | async-done | bytes 786464 | tf_op jit(solution)/shard_map/all_to_all | solution.py:338
  138.5 0.9 copy-done.1
  139.4 44.4 %block_back.1 = bf16[3072,128]{1,0:T(8,128)(2,1)} custom-call(s32[6144]{0:T(1024)} %squeeze.55.slot_ref, bf16[3072,128]{1,0:T(8,128)(2,1)} %bitcast.91, bf16[192,64]{1,0:T(8,128)(2,1)} %bitcast.111, bf16[64,64]{1,0:T(8,128)(2,1)} %bitcast.113, bf16[256,64]{1,0:T(8,128)(2,1)} %bitcast.107, bf16[64,256]{1,0:T(8,128)(2,1)} %get-tuple-element.16.down_ref, ...), custom_call_target="tpu_custom_call" | custom-call | flops 40000000000 | bytes 1000000 | tf_op jit(solution)/shard_map/block_back/pallas_call | solution.py:285
  183.9 4.3 %all-to-all-start.2 = ((bf16[128,24,128]{2,1,0:T(8,128)(2,1)}), bf16[128,24,128]{2,1,0:T(8,128)(2,1)S(1)}, u32[]{:S(2)}, u32[]{:S(2)}) async-start(bf16[128,24,128]{2,1,0:T(8,128)(2,1)} %bitcast.94), calls=%async_computation.2 | async-start | bytes 1572864 | tf_op jit(solution)/shard_map/all_to_all | solution.py:338
  188.8 16.1 %all-to-all-done.2 = bf16[128,24,128]{2,1,0:T(8,128)(2,1)S(1)} async-done(((bf16[128,24,128]{2,1,0:T(8,128)(2,1)}), bf16[128,24,128]{2,1,0:T(8,128)(2,1)S(1)}, u32[]{:S(2)}, u32[]{:S(2)}) %all-to-all-start.2) | async-done | bytes 786464 | tf_op jit(solution)/shard_map/all_to_all | solution.py:338
  205.0 0.9 copy-done.3
  205.9 9.8 %relay.1 = bf16[3072,128]{1,0:T(8,128)(2,1)} custom-call(s32[4096]{0:T(1024)} %fusion.34.place_ref.from_ref, s32[4096]{0:T(1024)} %fusion.37.to_ref, bf16[3072,128]{1,0:T(8,128)(2,1)} %bitcast.95), custom_call_target="tpu_custom_call" | custom-call | flops 1000000000 | bytes 1000000 | tf_op jit(solution)/shard_map/relay/pallas_call | solution.py:174
  215.7 4.2 %all-to-all-start.3 = ((bf16[128,24,128]{2,1,0:T(8,128)(2,1)}), bf16[128,24,128]{2,1,0:T(8,128)(2,1)S(1)}, u32[]{:S(2)}, u32[]{:S(2)}) async-start(bf16[128,24,128]{2,1,0:T(8,128)(2,1)} %bitcast.93), calls=%async_computation.3 | async-start | bytes 1572864 | tf_op jit(solution)/shard_map/all_to_all | solution.py:338
  224.2 12.5 %all-to-all-done.3 = bf16[128,24,128]{2,1,0:T(8,128)(2,1)S(1)} async-done(((bf16[128,24,128]{2,1,0:T(8,128)(2,1)}), bf16[128,24,128]{2,1,0:T(8,128)(2,1)S(1)}, u32[]{:S(2)}, u32[]{:S(2)}) %all-to-all-start.3) | async-done | bytes 786464 | tf_op jit(solution)/shard_map/all_to_all | solution.py:338
  236.7 0.9 copy-done.2
  237.5 38.0 %block_last.1 = bf16[64,4096]{1,0:T(8,128)(2,1)} custom-call(s32[6144]{0:T(1024)} %squeeze.54.slot_ref, bf16[3072,128]{1,0:T(8,128)(2,1)} %bitcast.92, bf16[192,64]{1,0:T(8,128)(2,1)} %bitcast.112, bf16[64,64]{1,0:T(8,128)(2,1)} %bitcast.114, bf16[256,64]{1,0:T(8,128)(2,1)} %bitcast.108, bf16[64,256]{1,0:T(8,128)(2,1)} %get-tuple-element.15.down_ref, ...), custom_call_target="tpu_custom_call" | custom-call | flops 40000000000 | bytes 1000000 | tf_op jit(solution)/shard_map/block_last/pallas_call | solution.py:285
  (101 shorter events, 17.4 us)
Async XLA Ops:
  3.1 1.4 copy-start.7
  4.5 12.8 %copy-start.16 = (s32[1,4,128]{2,1,0:T(4,128)S(1)}, s32[1,4,128]{2,1,0:T(4,128)}, u32[]{:S(2)}) copy-start(s32[1,4,128]{2,1,0:T(4,128)} %param.12) | copy-start | bytes 6148
  4.5 12.8 %copy-start.4 = (bf16[64,4096]{1,0:T(8,128)(2,1)S(1)}, bf16[64,4096]{1,0:T(8,128)(2,1)}, u32[]{:S(2)}) copy-start(bf16[64,4096]{1,0:T(8,128)(2,1)} %param.11) | copy-start | bytes 1572868
  5.8 104.2 %all-to-all-start = ((s32[128,1,96]{2,1,0:T(1,128)}), s32[128,1,96]{2,1,0:T(1,128)S(1)}, u32[]{:S(2)}, u32[]{:S(2)}) async-start(s32[128,1,96]{2,1,0:T(1,128)} %copy.71), calls=%async_computation | async-start | bytes 131072 | tf_op jit(solution)/shard_map/all_to_all | solution.py:362
  19.3 10.8 %copy-start.6 = (bf16[27,64,64]{2,1,0:T(8,128)(2,1)S(1)}, bf16[27,64,64]{2,1,0:T(8,128)(2,1)}, u32[]{:S(2)}) copy-start(bf16[27,64,64]{2,1,0:T(8,128)(2,1)} %param.16) | copy-start | bytes 663556
  19.4 14.4 %collective-permute-start = (bf16[64,128]{0,1:T(8,128)(2,1)S(1)}, bf16[64,128]{0,1:T(8,128)(2,1)S(1)}, u32[]{:S(2)}, u32[]{:S(2)}) collective-permute-start(bf16[64,128]{0,1:T(8,128)(2,1)S(1)} %get-tuple-element.14), channel_id=1, source_target_pairs={{0,16},{16,32},{32,48},{48,64},{64,80},{80,96},{96,112},{1,17},{17... | collective-permute-start | bytes 49160 | tf_op jit(solution)/shard_map/ppermute | solution.py:307
  23.1 10.7 %collective-permute-start.1 = (bf16[64,128]{0,1:T(8,128)(2,1)S(1)}, bf16[64,128]{0,1:T(8,128)(2,1)S(1)}, u32[]{:S(2)}, u32[]{:S(2)}) collective-permute-start(bf16[64,128]{0,1:T(8,128)(2,1)S(1)} %get-tuple-element.13), channel_id=1, source_target_pairs={{16,0},{32,16},{48,32},{64,48},{80,64},{96,80},{112,96},{17,1},{33... | collective-permute-start | bytes 49160 | tf_op jit(solution)/shard_map/ppermute | solution.py:308
  25.0 8.8 %collective-permute-start.2 = (bf16[64,128]{0,1:T(8,128)(2,1)S(1)}, bf16[64,128]{0,1:T(8,128)(2,1)S(1)}, u32[]{:S(2)}, u32[]{:S(2)}) collective-permute-start(bf16[64,128]{0,1:T(8,128)(2,1)S(1)} %get-tuple-element.12), channel_id=1, source_target_pairs={{0,1},{1,2},{2,3},{3,4},{4,5},{5,6},{6,7},{7,8},{8,9},{9,10},{10,1... | collective-permute-start | bytes 49160 | tf_op jit(solution)/shard_map/ppermute | solution.py:307
  28.1 5.8 %collective-permute-start.3 = (bf16[64,128]{0,1:T(8,128)(2,1)S(1)}, bf16[64,128]{0,1:T(8,128)(2,1)S(1)}, u32[]{:S(2)}, u32[]{:S(2)}) collective-permute-start(bf16[64,128]{0,1:T(8,128)(2,1)S(1)} %get-tuple-element.11), channel_id=1, source_target_pairs={{1,0},{2,1},{3,2},{4,3},{5,4},{6,5},{7,6},{8,7},{9,8},{10,9},{11,1... | collective-permute-start | bytes 49160 | tf_op jit(solution)/shard_map/ppermute | solution.py:308
  30.1 0.8 copy-start.17
  30.1 1.4 copy-start.5
  30.7 0.9 copy-start.11
  33.9 1.0 copy-start
  110.0 11.9 %copy-start.12 = (bf16[2,64,192]{2,1,0:T(8,128)(2,1)S(1)}, bf16[2,64,192]{2,1,0:T(8,128)(2,1)}, u32[]{:S(2)}) copy-start(bf16[2,64,192]{2,1,0:T(8,128)(2,1)} %param.17) | copy-start | bytes 147460
  110.0 14.8 %copy-start.15 = (bf16[2,64,64]{2,1,0:T(8,128)(2,1)S(1)}, bf16[2,64,64]{2,1,0:T(8,128)(2,1)}, u32[]{:S(2)}) copy-start(bf16[2,64,64]{2,1,0:T(8,128)(2,1)} %param.18) | copy-start | bytes 49156
  110.0 15.4 %copy-start.13 = (bf16[2,256,64]{1,2,0:T(8,128)(2,1)S(1)}, bf16[2,256,64]{1,2,0:T(8,128)(2,1)}, u32[]{:S(2)}) copy-start(bf16[2,256,64]{1,2,0:T(8,128)(2,1)} %param.20) | copy-start | bytes 196612
  110.0 28.5 %all-to-all-start.1 = ((bf16[128,24,128]{2,1,0:T(8,128)(2,1)}), bf16[128,24,128]{2,1,0:T(8,128)(2,1)S(1)}, u32[]{:S(2)}, u32[]{:S(2)}) async-start(bf16[128,24,128]{2,1,0:T(8,128)(2,1)} %bitcast.90), calls=%async_computation.1 | async-start | bytes 1572864 | tf_op jit(solution)/shard_map/all_to_all | solution.py:338
  138.5 0.9 copy-start.1
  183.9 4.3 %copy-start.8 = (s32[1,4096]{1,0:T(1,128)S(1)}, s32[1,4096]{1,0:T(1,128)}, u32[]{:S(2)}) copy-start(s32[1,4096]{1,0:T(1,128)} %copy-done.7) | copy-start | bytes 49156
  183.9 4.3 %copy-start.10 = (f32[32,128]{1,0:T(8,128)S(1)}, f32[32,128]{1,0:T(8,128)}, u32[]{:S(2)}) copy-start(f32[32,128]{1,0:T(8,128)} %copy-done.9) | copy-start | bytes 49156
  183.9 21.1 %all-to-all-start.2 = ((bf16[128,24,128]{2,1,0:T(8,128)(2,1)}), bf16[128,24,128]{2,1,0:T(8,128)(2,1)S(1)}, u32[]{:S(2)}, u32[]{:S(2)}) async-start(bf16[128,24,128]{2,1,0:T(8,128)(2,1)} %bitcast.94), calls=%async_computation.2 | async-start | bytes 1572864 | tf_op jit(solution)/shard_map/all_to_all | solution.py:338
  205.0 0.9 copy-start.3
  215.7 21.0 %all-to-all-start.3 = ((bf16[128,24,128]{2,1,0:T(8,128)(2,1)}), bf16[128,24,128]{2,1,0:T(8,128)(2,1)S(1)}, u32[]{:S(2)}, u32[]{:S(2)}) async-start(bf16[128,24,128]{2,1,0:T(8,128)(2,1)} %bitcast.93), calls=%async_computation.3 | async-start | bytes 1572864 | tf_op jit(solution)/shard_map/all_to_all | solution.py:338
  236.7 0.9 copy-start.2
  (2 other events, 1.5 us)
